TPU v7x, 32 devices: a whole 2x2x4 slice. The times are simulated.
32 devices in a mesh: space: 16 (over z, y, core), chan: 2 (over x).
Axes of the slice: x: 2, y: 2, z: 4, core: 2. Of those that a mesh axis runs over, the one named last changes fastest.
Arguments:
- inputs: bfloat16 [16, 256, 2048], P('space', 'chan'), may hold values from -6 to 6
- weights: bfloat16 [27, 256, 256], P(None, 'chan'), may hold values from -0.078125 to 0.078125
- cotangent: bfloat16 [16, 256, 2048], P('space', 'chan'), may hold values from -6 to 6
Outputs:
- output: bfloat16 [16, 256, 2048], P('space', 'chan')
- input_grad: bfloat16 [16, 256, 2048], P('space', 'chan')
- weight_grad: float32 [27, 256, 256], P(None, 'chan')
All inputs are finite; a program needn't handle non-finite values.
Results may differ from a plain program's by a relative error of at most 0.001.
Values may be sent and summed in bfloat16 or wider, within the bound.
A program may use at most 192 MiB of HBM per device.

v0:
```python
import jax
import jax.numpy as jnp
from jax import lax
from jax.sharding import PartitionSpec as P

PLANE_ROWS = 32
ROW_CELLS = 64


def extended(block, sides, width):
    for axis, dim in sides:
        count = lax.axis_size(axis)
        forward = [(i, i + 1) for i in range(count - 1)]
        backward = [(target, source) for source, target in forward]
        low = lax.ppermute(
            lax.slice_in_dim(block, block.shape[dim] - width, None, axis=dim), axis, forward
        )
        high = lax.ppermute(lax.slice_in_dim(block, 0, width, axis=dim), axis, backward)
        block = jnp.concatenate([low, block, high], axis=dim)
    return block


def plane_shift(field, tap_row, tap_col):
    lead = field.shape[:-1]
    grid = field.reshape(lead + (PLANE_ROWS, ROW_CELLS))
    padded = jnp.pad(grid, [(0, 0)] * len(lead) + [(1, 1), (1, 1)])
    window = padded[..., tap_row : tap_row + PLANE_ROWS, tap_col : tap_col + ROW_CELLS]
    return window.reshape(lead + (PLANE_ROWS * ROW_CELLS,))


def stack_at(padded, tap_row, tap_col):
    planes = padded.shape[0] - 2
    moved = plane_shift(padded, tap_row, tap_col)
    return jnp.concatenate(
        [moved[tap_depth : tap_depth + planes] for tap_depth in range(3)], axis=1
    )


def tap_weights(taps, tap_row, tap_col):
    return jnp.concatenate(
        [taps[tap_depth * 9 + tap_row * 3 + tap_col] for tap_depth in range(3)], axis=0
    )


def convolve(padded, taps):
    total = None
    for tap_row in range(3):
        for tap_col in range(3):
            term = jnp.einsum(
                "dcp,co->dop",
                stack_at(padded, tap_row, tap_col),
                tap_weights(taps, tap_row, tap_col),
                preferred_element_type=jnp.float32,
            )
            total = term if total is None else total + term
    return total


def weight_terms(padded, cot_whole, channels):
    pieces = [None] * 27
    for tap_row in range(3):
        for tap_col in range(3):
            block = jnp.einsum(
                "dcp,dop->co",
                stack_at(padded, tap_row, tap_col),
                cot_whole,
                preferred_element_type=jnp.float32,
            )
            block = block.reshape(3, channels, cot_whole.shape[1])
            for tap_depth in range(3):
                pieces[tap_depth * 9 + tap_row * 3 + tap_col] = block[tap_depth]
    return jnp.stack(pieces, axis=0)


def local(inputs, weights, cotangent):
    padded = extended(inputs, (("space", 0),), 1)
    partial_out = convolve(padded, weights)
    output = lax.psum_scatter(partial_out, "chan", scatter_dimension=1, tiled=True).astype(
        jnp.bfloat16
    )
    gathered = lax.all_gather(cotangent, "chan", axis=1, tiled=True)
    cot_padded = extended(gathered, (("space", 0),), 1)
    cot_whole = cot_padded[1:-1]
    flipped = jnp.transpose(weights[::-1], (0, 2, 1))
    input_grad = convolve(cot_padded, flipped).astype(jnp.bfloat16)
    local_terms = weight_terms(padded, cot_whole, inputs.shape[1])
    weight_grad = lax.psum(local_terms, "space")
    return (output, input_grad, weight_grad)


def solution(mesh):
    placed = (P("space", "chan", None), P(None, "chan", None), P("space", "chan", None))
    return jax.shard_map(
        local,
        mesh=mesh,
        in_specs=placed,
        out_specs=(P("space", "chan", None), P("space", "chan", None), P(None, "chan", None)),
        check_vma=False,
    )
```

profile of v0, /device:TPU:0, one launch (start us, length us, event | category | flops | bytes accessed | tf_op | source)
XLA Modules:
  0.0 200.8 jit_solution(18011192701551027474)
XLA Ops:
  7.2 1.4 copy.6
  8.7 1.3 collective-permute-start.1
  10.0 3.1 %collective-permute-start = (bf16[1,128,2048]{1,2,0:T(8,128)(2,1)S(1)}, bf16[1,128,2048]{1,2,0:T(8,128)(2,1)S(1)}, u32[]{:S(2)}, u32[]{:S(2)}) collective-permute-start(bf16[1,128,2048]{1,2,0:T(8,128)(2,1)S(1)} %copy.6), channel_id=1, source_target_pairs={{0,2},{2,4},{4,6},{6,8},{8,10},{10,12},{12,14},{14,16},{16,18},{18... | collective-permute-start | bytes 1572872 | tf_op jit(solution)/shard_map/ppermute | solution.py:15
  13.0 2.0 %copy.10 = bf16[1,128,2048]{1,2,0:T(8,128)(2,1)} copy(bf16[1,128,2048]{2,1,0:T(8,128)(2,1)} %param.5) | data formatting | bytes 1048576 | tf_op args[2]
  15.1 1.1 slice_bitcast_fusion.54
  16.4 0.8 slice_bitcast_fusion.47
  17.3 0.9 slice_bitcast_fusion.29
  19.2 0.7 pad_slice_fusion.25
  20.0 4.2 %pad_slice_fusion.26 = (bf16[1,128,32,64]{1,3,2,0:T(8,128)(2,1)S(1)}, bf16[1,128,32,64]{1,3,2,0:T(8,128)(2,1)S(1)}, bf16[1,128,32,64]{1,3,2,0:T(8,128)(2,1)S(1)}...) fusion(bf16[3,128,32,64]{1,3,2,0:T(8,128)(2,1)S(1)} %bitcast.377), kind=kLoop, calls=%fused_computation.131 | loop fusion | bytes 11534336 | tf_op jit(solution)/shard_map/slice | solution.py:35
  24.3 0.7 fusion.76
  25.1 0.7 fusion.75
  26.2 0.7 convolution_add_fusion.6
  27.0 0.8 convolution_add_fusion.5
  27.8 0.7 convolution_add_fusion.4
  29.0 0.8 fusion.46
  29.8 0.8 convolution_add_fusion.2
  30.6 0.8 convolution_add_fusion.1
  31.4 2.1 %fusion.45 = f32[1,256,2048]{2,1,0:T(8,128)} fusion(f32[256,2048]{1,0:T(8,128)S(1)} %convolution_add_fusion.1, bf16[1,128,2048]{1,2,0:T(8,128)(2,1)S(1)} %bitcast.408, bf16[1,128,2048]{1,2,0:T(8,128)(2,1)S(1)} %bitcast.406, bf16[1,128,2048]{1,2,0:T(8,128)(2,1)S(1)} %bitcast.378, bf16[128,256]{1,0:T(8,128)(2,1)S(1)} %get-tuple-element.73, ...), kind=kOutput, calls=%fused_computation.56 | convolution fusion | flops 408485888 | bytes 5963776 | tf_op jit(solution)/shard_map/dcp,co->dop/dot_general | solution.py:49
  33.8 6.0 %all-gather.2.cloned.1.call-done = bf16[1,256,2048]{1,2,0:T(8,128)(2,1)} async-done(((bf16[1,128,2048]{1,2,0:T(8,128)(2,1)}), bf16[1,256,2048]{1,2,0:T(8,128)(2,1)}) %all-gather.2.cloned.1.call-update) | async-done | bytes 1048592 | tf_op jit(solution)/shard_map/all_gather | solution.py:81
  39.8 2.4 %fusion.73 = f32[384,256]{1,0:T(8,128)S(1)} fusion(bf16[1,256,2048]{1,2,0:T(8,128)(2,1)} %all-gather.2.cloned.1.call-done, bf16[1,128,2048]{1,2,0:T(8,128)(2,1)} %bitcast.447, bf16[1,128,2048]{1,2,0:T(8,128)(2,1)} %bitcast.445, bf16[1,128,2048]{1,2,0:T(8,128)(2,1)} %bitcast.449), kind=kOutput, calls=%fused_computation.101 | convolution fusion | flops 407371776 | bytes 3014656 | tf_op jit(solution)/shard_map/dcp,dop->co/dot_general | solution.py:63
  42.2 0.7 fusion.193
  42.9 1.9 fusion.71
  44.9 0.7 fusion.192
  45.6 1.9 fusion.69
  47.5 0.7 fusion.191
  48.2 2.1 %fusion.67 = f32[384,256]{1,0:T(8,128)S(1)} fusion(bf16[1,256,2048]{1,2,0:T(8,128)(2,1)} %all-gather.2.cloned.1.call-done, bf16[1,128,2048]{1,2,0:T(8,128)(2,1)S(1)} %bitcast.393, bf16[1,128,2048]{1,2,0:T(8,128)(2,1)S(1)} %bitcast.391, bf16[1,128,2048]{1,2,0:T(8,128)(2,1)S(1)} %bitcast.389), kind=kOutput, calls=%fused_computation.95 | convolution fusion | flops 407371776 | bytes 3014656 | tf_op jit(solution)/shard_map/dcp,dop->co/dot_general | solution.py:63
  50.4 0.7 fusion.190
  51.1 1.9 fusion.65
  53.0 0.7 fusion.189
  53.7 1.8 fusion.63
  55.5 0.7 fusion.188
  56.2 1.9 fusion.61
  58.1 0.7 fusion.187
  58.8 1.9 fusion.59
  60.7 0.7 fusion.186
  61.4 1.8 fusion.57
  63.3 0.7 fusion.185
  63.9 1.3 collective-permute-start.3
  65.2 5.2 %collective-permute-start.2 = (bf16[1,256,2048]{1,2,0:T(8,128)(2,1)}, bf16[1,256,2048]{1,2,0:T(8,128)(2,1)}, u32[]{:S(2)}, u32[]{:S(2)}) collective-permute-start(bf16[1,256,2048]{1,2,0:T(8,128)(2,1)} %all-gather.2.cloned.1.call-done), channel_id=1, source_target_pairs={{0,2},{2,4},{4,6},{6,8},{8,10},{10,12},{12,14},{14,16},{16,18},{18... | collective-permute-start | bytes 3145736 | tf_op jit(solution)/shard_map/ppermute | solution.py:15
  70.4 0.7 fusion.184
  71.0 0.7 fusion.183
  71.7 0.7 fusion.182
  72.4 0.7 fusion.181
  73.0 0.7 fusion.180
  74.4 0.7 fusion.178
  75.7 0.7 fusion.176
  77.0 0.7 fusion.174
  78.4 0.7 fusion.172
  82.4 1.0 copy-done.41
  83.3 2.2 %pad_maximum_fusion = bf16[3,256,2048]{1,2,0:T(8,128)(2,1)S(1)} fusion(bf16[1,256,2048]{1,2,0:T(8,128)(2,1)} %copy-done.41, bf16[1,256,2048]{1,2,0:T(8,128)(2,1)} %all-gather.2.cloned.1.call-done, bf16[1,256,2048]{1,2,0:T(8,128)(2,1)} %collective-permute-done.2), kind=kLoop, calls=%fused_computation | loop fusion | flops 3145728 | bytes 6291456 | tf_op jit(solution)/shard_map/concatenate | solution.py:19
  85.5 3.5 %pad_slice_fusion.1 = (bf16[1,256,32,64]{1,3,2,0:T(8,128)(2,1)}, bf16[1,256,32,64]{1,3,2,0:T(8,128)(2,1)}, bf16[1,256,32,64]{1,3,2,0:T(8,128)(2,1)}, bf16[1,256,32,64]{1,3,2,0:T(8,128)(2,1)}, bf16[1,256,32,64]{1,3,2,0:T(8,128)(2,1)}) fusion(bf16[3,256,32,64]{1,3,2,0:T(8,128)(2,1)S(1)} %bitcast.374), kind=kLoop, calls=%fused_computation.106 | loop fusion | bytes 8388608 | tf_op jit(solution)/shard_map/slice | solution.py:35
  89.0 9.7 %pad_slice_fusion.2 = (bf16[1,256,32,64]{1,3,2,0:T(8,128)(2,1)S(1)}, bf16[1,256,32,64]{1,3,2,0:T(8,128)(2,1)}, bf16[1,256,32,64]{1,3,2,0:T(8,128)(2,1)}, bf16[1,...) fusion(bf16[3,256,32,64]{1,3,2,0:T(8,128)(2,1)S(1)} %bitcast.375), kind=kLoop, calls=%fused_computation.107 | loop fusion | bytes 23068672 | tf_op jit(solution)/shard_map/slice | solution.py:35
  98.7 3.2 %fusion = f32[128,2048]{1,0:T(8,128)S(1)} fusion(bf16[1,256,2048]{1,2,0:T(8,128)(2,1)} %bitcast.432, bf16[1,256,2048]{1,2,0:T(8,128)(2,1)} %bitcast.431, bf16[1,256,2048]{1,2,0:T(8,128)(2,1)} %bitcast.437, bf16[256,128]{0,1:T(8,128)(2,1)S(1)} %copy-done.67, bf16[256,128]{0,1:T(8,128)(2,1)} %get-tuple-element.52, bf16[256,128]{0,1:T(8,128)(2,1)} %get-tuple-element.53), kind=kOutput, calls=%fused_computation.2 | convolution fusion | flops 412680192 | bytes 4390912 | tf_op jit(solution)/shard_map/dcp,co->dop/dot_general | solution.py:49
  102.1 1.1 fusion.53
  104.0 1.1 fusion.52
  105.5 1.1 fusion.51
  106.8 1.1 fusion.25
  108.0 2.7 %fusion.54 = f32[128,2048]{1,0:T(8,128)S(1)} fusion(f32[128,2048]{1,0:T(8,128)S(1)} %fusion.25, f32[128,2048]{1,0:T(8,128)S(1)} %fusion.51, bf16[1,256,2048]{1,2,0:T(8,128)(2,1)S(1)} %copy-done.42, bf16[1,256,2048]{1,2,0:T(8,128)(2,1)} %all-gather.2.cloned.1.call-done, bf16[1,256,2048]{1,2,0:T(8,128)(2,1)} %collective-permute-done.2, ...), kind=kOutput, calls=%fused_computation.71 | convolution fusion | flops 413204480 | bytes 6488064 | tf_op jit(solution)/shard_map/dcp,co->dop/dot_general | solution.py:49
  110.8 1.1 fusion.49
  112.3 1.1 fusion.48
  113.9 1.9 fusion.56
  115.8 2.1 %convert_element_type.38 = bf16[1,128,2048]{2,1,0:T(8,128)(2,1)} convert(f32[1,128,2048]{2,1,0:T(8,128)} %reduce-scatter.2.cloned.1.call-done) | non-fusion elementwise | flops 262144 | bytes 1572864 | tf_op jit(solution)/shard_map/convert_element_type | solution.py:78
  117.9 72.2 %all-reduce.4.cloned.1.call-done = f32[27,128,256]{2,1,0:T(8,128)} async-done(((f32[27,128,256]{2,1,0:T(8,128)}), f32[27,128,256]{2,1,0:T(8,128)}) %all-reduce.4.cloned.1.call-update) | async-done | bytes 3538960 | tf_op jit(solution)/shard_map/psum | solution.py:87
  190.1 4.2 %copy.38 = f32[27,128,256]{2,1,0:T(8,128)} copy(f32[27,128,256]{2,1,0:T(8,128)} %all-reduce.4.cloned.1.call-done) | data formatting | bytes 7077888
  (172 shorter events, 10.3 us)
Async XLA Ops:
  7.2 9.1 %copy-start = (bf16[27,128,256]{2,1,0:T(8,128)(2,1)S(1)}, bf16[27,128,256]{2,1,0:T(8,128)(2,1)}, u32[]{:S(2)}) copy-start(bf16[27,128,256]{2,1,0:T(8,128)(2,1)} %param.4) | copy-start | bytes 5308420
  7.2 32.6 %all-gather.2.cloned.1.call-start = ((), (), s32[]{:S(2)}) async-start(), calls=%async_computation.2 | async-start | bytes 1572864 | tf_op jit(solution)/shard_map/all_gather | solution.py:81
  8.7 9.6 %collective-permute-start.1 = (bf16[1,128,2048]{1,2,0:T(8,128)(2,1)S(1)}, bf16[1,128,2048]{1,2,0:T(8,128)(2,1)S(1)}, u32[]{:S(2)}, u32[]{:S(2)}) collective-permute-start(bf16[1,128,2048]{1,2,0:T(8,128)(2,1)S(1)} %copy.6), channel_id=1, source_target_pairs={{2,0},{4,2},{6,4},{8,6},{10,8},{12,10},{14,12},{16,14},{18,16},{20... | collective-permute-start | bytes 1572872 | tf_op jit(solution)/shard_map/ppermute | solution.py:18
  10.0 8.3 %collective-permute-start = (bf16[1,128,2048]{1,2,0:T(8,128)(2,1)S(1)}, bf16[1,128,2048]{1,2,0:T(8,128)(2,1)S(1)}, u32[]{:S(2)}, u32[]{:S(2)}) collective-permute-start(bf16[1,128,2048]{1,2,0:T(8,128)(2,1)S(1)} %copy.6), channel_id=1, source_target_pairs={{0,2},{2,4},{4,6},{6,8},{8,10},{10,12},{12,14},{14,16},{16,18},{18... | collective-permute-start | bytes 1572872 | tf_op jit(solution)/shard_map/ppermute | solution.py:15
  15.1 100.7 %reduce-scatter.2.cloned.1.call-start = ((), (), s32[]{:S(2)}) async-start(), calls=%async_computation.1 | async-start | bytes 3145728 | tf_op jit(solution)/shard_map/reduce_scatter | solution.py:78
  19.9 4.4 %copy-start.55 = (bf16[1,128,32,64]{1,3,2,0:T(8,128)(2,1)}, bf16[1,128,32,64]{1,3,2,0:T(8,128)(2,1)S(1)}, u32[]{:S(2)}) copy-start(bf16[1,128,32,64]{1,3,2,0:T(8,128)(2,1)S(1)} %get-tuple-element.104) | copy-start | bytes 1572868
  20.0 10.6 %copy-start.23 = (bf16[1,128,32,64]{1,3,2,0:T(8,128)(2,1)}, bf16[1,128,32,64]{1,3,2,0:T(8,128)(2,1)S(1)}, u32[]{:S(2)}) copy-start(bf16[1,128,32,64]{1,3,2,0:T(8,128)(2,1)S(1)} %get-tuple-element.101) | copy-start | bytes 1572868
  20.0 10.6 %copy-start.25 = (bf16[1,128,32,64]{1,3,2,0:T(8,128)(2,1)}, bf16[1,128,32,64]{1,3,2,0:T(8,128)(2,1)S(1)}, u32[]{:S(2)}) copy-start(bf16[1,128,32,64]{1,3,2,0:T(8,128)(2,1)S(1)} %get-tuple-element.102) | copy-start | bytes 1572868
  20.0 11.4 %copy-start.19 = (bf16[1,128,32,64]{1,3,2,0:T(8,128)(2,1)}, bf16[1,128,32,64]{1,3,2,0:T(8,128)(2,1)S(1)}, u32[]{:S(2)}) copy-start(bf16[1,128,32,64]{1,3,2,0:T(8,128)(2,1)S(1)} %get-tuple-element.100) | copy-start | bytes 1572868
  20.0 11.4 %copy-start.21 = (bf16[1,128,32,64]{1,3,2,0:T(8,128)(2,1)}, bf16[1,128,32,64]{1,3,2,0:T(8,128)(2,1)S(1)}, u32[]{:S(2)}) copy-start(bf16[1,128,32,64]{1,3,2,0:T(8,128)(2,1)S(1)} %get-tuple-element.103) | copy-start | bytes 1572868
  24.2 1.7 copy-start.47
  24.2 1.7 copy-start.49
  24.2 1.7 copy-start.51
  24.2 1.7 copy-start.53
  24.2 1.7 copy-start.54
  24.2 1.7 copy-start.13
  24.3 1.8 copy-start.15
  24.3 1.9 copy-start.17
  24.3 2.7 %copy-start.7 = (bf16[1,128,32,64]{1,3,2,0:T(8,128)(2,1)}, bf16[1,128,32,64]{1,3,2,0:T(8,128)(2,1)S(1)}, u32[]{:S(2)}) copy-start(bf16[1,128,32,64]{1,3,2,0:T(8,128)(2,1)S(1)} %get-tuple-element.87) | copy-start | bytes 1572868
  24.3 2.7 %copy-start.9 = (bf16[1,128,32,64]{1,3,2,0:T(8,128)(2,1)}, bf16[1,128,32,64]{1,3,2,0:T(8,128)(2,1)S(1)}, u32[]{:S(2)}) copy-start(bf16[1,128,32,64]{1,3,2,0:T(8,128)(2,1)S(1)} %get-tuple-element.88) | copy-start | bytes 1572868
  24.3 2.7 %copy-start.11 = (bf16[1,128,32,64]{1,3,2,0:T(8,128)(2,1)}, bf16[1,128,32,64]{1,3,2,0:T(8,128)(2,1)S(1)}, u32[]{:S(2)}) copy-start(bf16[1,128,32,64]{1,3,2,0:T(8,128)(2,1)S(1)} %get-tuple-element.89) | copy-start | bytes 1572868
  24.3 3.5 %copy-start.1 = (bf16[1,128,32,64]{1,3,2,0:T(8,128)(2,1)}, bf16[1,128,32,64]{1,3,2,0:T(8,128)(2,1)S(1)}, u32[]{:S(2)}) copy-start(bf16[1,128,32,64]{1,3,2,0:T(8,128)(2,1)S(1)} %get-tuple-element.90) | copy-start | bytes 1572868
  24.3 3.5 %copy-start.3 = (bf16[1,128,32,64]{1,3,2,0:T(8,128)(2,1)}, bf16[1,128,32,64]{1,3,2,0:T(8,128)(2,1)S(1)}, u32[]{:S(2)}) copy-start(bf16[1,128,32,64]{1,3,2,0:T(8,128)(2,1)S(1)} %get-tuple-element.91) | copy-start | bytes 1572868
  24.3 3.5 %copy-start.5 = (bf16[1,128,32,64]{1,3,2,0:T(8,128)(2,1)}, bf16[1,128,32,64]{1,3,2,0:T(8,128)(2,1)S(1)}, u32[]{:S(2)}) copy-start(bf16[1,128,32,64]{1,3,2,0:T(8,128)(2,1)S(1)} %get-tuple-element.92) | copy-start | bytes 1572868
  33.5 156.6 %all-reduce.4.cloned.1.call-start = ((), (), s32[]{:S(2)}) async-start(), calls=%async_computation.3 | async-start | bytes 7077888 | tf_op jit(solution)/shard_map/psum | solution.py:87
  39.8 3.1 %copy-start.14 = (bf16[1,128,32,64]{1,3,2,0:T(8,128)(2,1)S(1)}, bf16[1,128,32,64]{1,3,2,0:T(8,128)(2,1)}, u32[]{:S(2)}) copy-start(bf16[1,128,32,64]{1,3,2,0:T(8,128)(2,1)} %copy-done.13) | copy-start | bytes 1572868
  39.8 3.1 %copy-start.16 = (bf16[1,128,32,64]{1,3,2,0:T(8,128)(2,1)S(1)}, bf16[1,128,32,64]{1,3,2,0:T(8,128)(2,1)}, u32[]{:S(2)}) copy-start(bf16[1,128,32,64]{1,3,2,0:T(8,128)(2,1)} %copy-done.15) | copy-start | bytes 1572868
  39.8 3.1 %copy-start.18 = (bf16[1,128,32,64]{1,3,2,0:T(8,128)(2,1)S(1)}, bf16[1,128,32,64]{1,3,2,0:T(8,128)(2,1)}, u32[]{:S(2)}) copy-start(bf16[1,128,32,64]{1,3,2,0:T(8,128)(2,1)} %copy-done.17) | copy-start | bytes 1572868
  42.9 2.6 %copy-start.8 = (bf16[1,128,32,64]{1,3,2,0:T(8,128)(2,1)S(1)}, bf16[1,128,32,64]{1,3,2,0:T(8,128)(2,1)}, u32[]{:S(2)}) copy-start(bf16[1,128,32,64]{1,3,2,0:T(8,128)(2,1)} %copy-done.7) | copy-start | bytes 1572868
  42.9 2.6 %copy-start.10 = (bf16[1,128,32,64]{1,3,2,0:T(8,128)(2,1)S(1)}, bf16[1,128,32,64]{1,3,2,0:T(8,128)(2,1)}, u32[]{:S(2)}) copy-start(bf16[1,128,32,64]{1,3,2,0:T(8,128)(2,1)} %copy-done.9) | copy-start | bytes 1572868
  42.9 2.6 %copy-start.12 = (bf16[1,128,32,64]{1,3,2,0:T(8,128)(2,1)S(1)}, bf16[1,128,32,64]{1,3,2,0:T(8,128)(2,1)}, u32[]{:S(2)}) copy-start(bf16[1,128,32,64]{1,3,2,0:T(8,128)(2,1)} %copy-done.11) | copy-start | bytes 1572868
  45.6 2.7 %copy-start.2 = (bf16[1,128,32,64]{1,3,2,0:T(8,128)(2,1)S(1)}, bf16[1,128,32,64]{1,3,2,0:T(8,128)(2,1)}, u32[]{:S(2)}) copy-start(bf16[1,128,32,64]{1,3,2,0:T(8,128)(2,1)} %copy-done.1) | copy-start | bytes 1572868
  45.6 2.6 %copy-start.4 = (bf16[1,128,32,64]{1,3,2,0:T(8,128)(2,1)S(1)}, bf16[1,128,32,64]{1,3,2,0:T(8,128)(2,1)}, u32[]{:S(2)}) copy-start(bf16[1,128,32,64]{1,3,2,0:T(8,128)(2,1)} %copy-done.3) | copy-start | bytes 1572868
  45.6 2.6 %copy-start.6 = (bf16[1,128,32,64]{1,3,2,0:T(8,128)(2,1)S(1)}, bf16[1,128,32,64]{1,3,2,0:T(8,128)(2,1)}, u32[]{:S(2)}) copy-start(bf16[1,128,32,64]{1,3,2,0:T(8,128)(2,1)} %copy-done.5) | copy-start | bytes 1572868
  48.2 2.8 %copy-start.29 = (bf16[1,128,2048]{1,2,0:T(8,128)(2,1)S(1)}, bf16[1,128,2048]{1,2,0:T(8,128)(2,1)}, u32[]{:S(2)}) copy-start(bf16[1,128,2048]{1,2,0:T(8,128)(2,1)} %copy-done.27) | copy-start | bytes 1572868
  48.2 2.8 %copy-start.32 = (bf16[1,128,2048]{1,2,0:T(8,128)(2,1)S(1)}, bf16[1,128,2048]{1,2,0:T(8,128)(2,1)}, u32[]{:S(2)}) copy-start(bf16[1,128,2048]{1,2,0:T(8,128)(2,1)} %copy-done.30) | copy-start | bytes 1572868
  51.1 2.6 %copy-start.48 = (bf16[1,128,32,64]{1,3,2,0:T(8,128)(2,1)S(1)}, bf16[1,128,32,64]{1,3,2,0:T(8,128)(2,1)}, u32[]{:S(2)}) copy-start(bf16[1,128,32,64]{1,3,2,0:T(8,128)(2,1)} %copy-done.47) | copy-start | bytes 1572868
  51.1 2.6 %copy-start.50 = (bf16[1,128,32,64]{1,3,2,0:T(8,128)(2,1)S(1)}, bf16[1,128,32,64]{1,3,2,0:T(8,128)(2,1)}, u32[]{:S(2)}) copy-start(bf16[1,128,32,64]{1,3,2,0:T(8,128)(2,1)} %copy-done.49) | copy-start | bytes 1572868
  51.1 2.6 %copy-start.52 = (bf16[1,128,32,64]{1,3,2,0:T(8,128)(2,1)S(1)}, bf16[1,128,32,64]{1,3,2,0:T(8,128)(2,1)}, u32[]{:S(2)}) copy-start(bf16[1,128,32,64]{1,3,2,0:T(8,128)(2,1)} %copy-done.51) | copy-start | bytes 1572868
  56.2 2.6 %copy-start.24 = (bf16[1,128,32,64]{1,3,2,0:T(8,128)(2,1)S(1)}, bf16[1,128,32,64]{1,3,2,0:T(8,128)(2,1)}, u32[]{:S(2)}) copy-start(bf16[1,128,32,64]{1,3,2,0:T(8,128)(2,1)} %copy-done.23) | copy-start | bytes 1572868
  56.2 2.6 %copy-start.26 = (bf16[1,128,32,64]{1,3,2,0:T(8,128)(2,1)S(1)}, bf16[1,128,32,64]{1,3,2,0:T(8,128)(2,1)}, u32[]{:S(2)}) copy-start(bf16[1,128,32,64]{1,3,2,0:T(8,128)(2,1)} %copy-done.25) | copy-start | bytes 1572868
  58.8 2.6 %copy-start.20 = (bf16[1,128,32,64]{1,3,2,0:T(8,128)(2,1)S(1)}, bf16[1,128,32,64]{1,3,2,0:T(8,128)(2,1)}, u32[]{:S(2)}) copy-start(bf16[1,128,32,64]{1,3,2,0:T(8,128)(2,1)} %copy-done.19) | copy-start | bytes 1572868
  58.8 2.6 %copy-start.22 = (bf16[1,128,32,64]{1,3,2,0:T(8,128)(2,1)S(1)}, bf16[1,128,32,64]{1,3,2,0:T(8,128)(2,1)}, u32[]{:S(2)}) copy-start(bf16[1,128,32,64]{1,3,2,0:T(8,128)(2,1)} %copy-done.21) | copy-start | bytes 1572868
  63.9 18.4 %collective-permute-start.3 = (bf16[1,256,2048]{1,2,0:T(8,128)(2,1)}, bf16[1,256,2048]{1,2,0:T(8,128)(2,1)S(1)}, u32[]{:S(2)}, u32[]{:S(2)}) collective-permute-start(bf16[1,256,2048]{1,2,0:T(8,128)(2,1)} %all-gather.2.cloned.1.call-done), channel_id=1, source_target_pairs={{2,0},{4,2},{6,4},{8,6},{10,8},{12,10},{14,12},{16,14},{18,16},{20... | collective-permute-start | bytes 3145736 | tf_op jit(solution)/shard_map/ppermute | solution.py:18
  65.2 18.1 %collective-permute-start.2 = (bf16[1,256,2048]{1,2,0:T(8,128)(2,1)}, bf16[1,256,2048]{1,2,0:T(8,128)(2,1)}, u32[]{:S(2)}, u32[]{:S(2)}) collective-permute-start(bf16[1,256,2048]{1,2,0:T(8,128)(2,1)} %all-gather.2.cloned.1.call-done), channel_id=1, source_target_pairs={{0,2},{2,4},{4,6},{6,8},{8,10},{10,12},{12,14},{14,16},{16,18},{18... | collective-permute-start | bytes 3145736 | tf_op jit(solution)/shard_map/ppermute | solution.py:15
  89.0 9.7 %copy-start.67 = (bf16[256,128]{0,1:T(8,128)(2,1)S(1)}, bf16[256,128]{0,1:T(8,128)(2,1)}, u32[]{:S(2)}) copy-start(bf16[256,128]{0,1:T(8,128)(2,1)} %get-tuple-element.51) | copy-start | bytes 196612
  98.7 3.3 %copy-start.38 = (bf16[1,256,32,64]{1,3,2,0:T(8,128)(2,1)S(1)}, bf16[1,256,32,64]{1,3,2,0:T(8,128)(2,1)}, u32[]{:S(2)}) copy-start(bf16[1,256,32,64]{1,3,2,0:T(8,128)(2,1)} %get-tuple-element.6) | copy-start | bytes 3145732
  98.7 3.3 %copy-start.39 = (bf16[1,256,32,64]{1,3,2,0:T(8,128)(2,1)S(1)}, bf16[1,256,32,64]{1,3,2,0:T(8,128)(2,1)}, u32[]{:S(2)}) copy-start(bf16[1,256,32,64]{1,3,2,0:T(8,128)(2,1)} %get-tuple-element.7) | copy-start | bytes 3145732
  98.7 3.3 %copy-start.40 = (bf16[1,256,32,64]{1,3,2,0:T(8,128)(2,1)S(1)}, bf16[1,256,32,64]{1,3,2,0:T(8,128)(2,1)}, u32[]{:S(2)}) copy-start(bf16[1,256,32,64]{1,3,2,0:T(8,128)(2,1)} %get-tuple-element.8) | copy-start | bytes 3145732
  98.7 3.3 %copy-start.61 = (bf16[256,128]{0,1:T(8,128)(2,1)S(1)}, bf16[256,128]{0,1:T(8,128)(2,1)}, u32[]{:S(2)}) copy-start(bf16[256,128]{0,1:T(8,128)(2,1)} %get-tuple-element.48) | copy-start | bytes 196612
  98.7 3.3 %copy-start.62 = (bf16[256,128]{0,1:T(8,128)(2,1)S(1)}, bf16[256,128]{0,1:T(8,128)(2,1)}, u32[]{:S(2)}) copy-start(bf16[256,128]{0,1:T(8,128)(2,1)} %get-tuple-element.49) | copy-start | bytes 196612
  98.7 3.3 %copy-start.63 = (bf16[256,128]{0,1:T(8,128)(2,1)S(1)}, bf16[256,128]{0,1:T(8,128)(2,1)}, u32[]{:S(2)}) copy-start(bf16[256,128]{0,1:T(8,128)(2,1)} %get-tuple-element.50) | copy-start | bytes 196612
  102.0 1.6 copy-start.36
  102.1 1.9 copy-start.37
  102.1 1.9 copy-start.56
  102.1 1.9 copy-start.57
  102.1 1.9 copy-start.74
  104.0 1.5 copy-start.34
  104.0 1.5 copy-start.71
  108.0 2.8 %copy-start.58 = (bf16[256,128]{0,1:T(8,128)(2,1)S(1)}, bf16[256,128]{0,1:T(8,128)(2,1)}, u32[]{:S(2)}) copy-start(bf16[256,128]{0,1:T(8,128)(2,1)} %get-tuple-element.33) | copy-start | bytes 196612
  108.0 2.8 %copy-start.59 = (bf16[256,128]{0,1:T(8,128)(2,1)S(1)}, bf16[256,128]{0,1:T(8,128)(2,1)}, u32[]{:S(2)}) copy-start(bf16[256,128]{0,1:T(8,128)(2,1)} %get-tuple-element.34) | copy-start | bytes 196612
  108.0 2.8 %copy-start.60 = (bf16[256,128]{0,1:T(8,128)(2,1)S(1)}, bf16[256,128]{0,1:T(8,128)(2,1)}, u32[]{:S(2)}) copy-start(bf16[256,128]{0,1:T(8,128)(2,1)} %get-tuple-element.35) | copy-start | bytes 196612
  110.8 1.6 copy-start.46
  112.3 1.6 copy-start.44
  (18 other events, 21.4 us)
Sparse Core Ops, SparseCore 0:
  15.2 24.5 all-gather.1
  42.0 32.3 reduce-scatter.1
  82.5 107.5 all-reduce.3
where the time goes:
time: 202 us; the launch traced here: 201 us
  waiting for transfers between devices  78.3 us (39%)
  local copies, waits for them, and re-layouts  51.3 us (25%)
  matrix products  40.9 us (20%)
  between operations  14.8 us (7%)
  starting transfers between devices  11.1 us (5%)
  other arithmetic  4.45 us (2%)
    psum x1, waiting for transfers between devices, local(): weight_grad = lax.psum(local_terms, 'space')  72.2 us
    unnamed x179, local copies, waits for them, and re-layouts  29.5 us
    dot_general x18, matrix products, convolve(): jnp.einsum('dcp,co->dop', stack_at(padded, tap_row, tap_col), tap_weights...  23 us
    slice x4, local copies, waits for them, and re-layouts, stack_at(): moved[tap_depth:tap_depth + planes]  18.1 us
    dot_general x9, matrix products, weight_terms(): jnp.einsum('dcp,dop->co', stack_at(padded, tap_row, tap_col), cot_whole,...  17.9 us
    ppermute x2, starting transfers between devices, extended(): lax.ppermute(lax.slice_in_dim(block, block.shape[dim] - width, None, axis...  8.24 us
    all_gather x1, waiting for transfers between devices, local(): gathered = lax.all_gather(cotangent, 'chan', axis=1, tiled=True)  6.04 us
  transfers between devices with their start and end apart: 7, of which 2 were waited for; matrix products, arithmetic and copies ran while one was open for 43% of the time, Pallas kernels for 0%

commit v1 on v0

--- a/solution.py
+++ b/solution.py
@@ -1,7 +1,15 @@
+import functools
+
 import jax
 import jax.numpy as jnp
 from jax import lax
+from jax.experimental import pallas as pl
+from jax.experimental.pallas import tpu as pltpu
 from jax.sharding import PartitionSpec as P
+
+MESH = pl.DeviceIdType.MESH
+F32 = jnp.float32
+BF16 = jnp.bfloat16
 
 PLANE_ROWS = 32
 ROW_CELLS = 64
@@ -88,10 +96,332 @@
     return (output, input_grad, weight_grad)
 
 
+TAPS = 9
+
+
+def moved(value, rows, cols):
+    cells = value.shape[-1]
+    shift = rows * ROW_CELLS + cols
+    if shift == 0:
+        return value
+    at = lax.broadcasted_iota(jnp.int32, value.shape, value.ndim - 1)
+    out = pltpu.roll(value, shift % cells, value.ndim - 1)
+    keep = None
+    if rows == 1:
+        keep = at >= ROW_CELLS
+    elif rows == -1:
+        keep = at < cells - ROW_CELLS
+    if cols != 0:
+        col = at % ROW_CELLS
+        side = col != (0 if cols == 1 else ROW_CELLS - 1)
+        keep = side if keep is None else keep & side
+    return jnp.where(keep, out, jnp.zeros_like(out))
+
+
+def kernel(
+    count, levels, x_ref, w_ref, cot_ref, out_ref, grad_ref, wg_ref,
+    x3, c3, wf, cs, z, mine, theirs, rx, part, *rest,
+):
+    bufs, (hs, hr, gs, gr) = rest[:levels], rest[levels:]
+    s = lax.axis_index("space")
+    h = lax.axis_index("chan")
+    other = 1 - h
+    ci, cells = x_ref.shape
+    co = wg_ref.shape[2]
+    rows3 = 3 * ci
+    has_prev, has_next = s > 0, s < count - 1
+    prev, nxt = jnp.maximum(s - 1, 0), jnp.minimum(s + 1, count - 1)
+    bits = [(s // (1 << b)) % 2 for b in range(levels)]
+    mates = [s + (1 - 2 * bits[b]) * (1 << b) for b in range(levels)]
+    partner = (s, other)
+
+    barrier = pltpu.get_barrier_semaphore()
+    for b in range(levels):
+        pl.semaphore_signal(barrier, inc=1, device_id=(mates[b], h), device_id_type=MESH)
+    pl.semaphore_signal(barrier, inc=1, device_id=partner, device_id_type=MESH)
+
+    for near in ((s + 1) % count, (s + count - 1) % count):
+        pl.semaphore_signal(barrier, inc=1, device_id=(near, h), device_id_type=MESH)
+    pl.semaphore_wait(barrier, levels + 3)
+
+    def remote(src, dst, i, device):
+        return pltpu.make_async_remote_copy(
+            src_ref=src, dst_ref=dst, send_sem=hs.at[i], recv_sem=hr.at[i],
+            device_id=device, device_id_type=MESH,
+        )
+
+    def half_at(block, which):
+        return pl.ds(pl.multiple_of(block * co + which * ci, ci), ci)
+
+    cot_x = remote(cot_ref, c3.at[half_at(1, h)], 0, partner)
+    x_next = remote(x_ref, x3.at[pl.ds(0, ci)], 1, (nxt, h))
+    x_prev = remote(x_ref, x3.at[pl.ds(2 * ci, ci)], 2, (prev, h))
+    c_next = remote(cot_ref, c3.at[half_at(2, h)], 3, (nxt, h))
+    c_prev = remote(cot_ref, c3.at[half_at(0, h)], 4, (prev, h))
+    gathered = c3.at[half_at(1, other)]
+    f_next = remote(gathered, c3.at[half_at(2, other)], 5, (nxt, h))
+    f_prev = remote(gathered, c3.at[half_at(0, other)], 6, (prev, h))
+    share = remote(theirs, rx, 7, partner)
+
+    cot_x.start()
+
+    @pl.when(has_next)
+    def _():
+        x_next.start()
+
+    @pl.when(has_prev)
+    def _():
+        x_prev.start()
+
+    @pl.when(has_next)
+    def _():
+        c_next.start()
+
+    @pl.when(has_prev)
+    def _():
+        c_prev.start()
+
+    x3[pl.ds(ci, ci), :] = x_ref[...]
+    c3[half_at(1, h), :] = cot_ref[...]
+
+    @pl.when(s == 0)
+    def _():
+        x3[pl.ds(0, ci), :] = jnp.zeros((ci, cells), BF16)
+        c3[pl.ds(2 * co, co), :] = jnp.zeros((co, cells), BF16)
+
+    @pl.when(s == count - 1)
+    def _():
+        x3[pl.ds(2 * ci, ci), :] = jnp.zeros((ci, cells), BF16)
+        c3[pl.ds(0, co), :] = jnp.zeros((co, cells), BF16)
+
+    @pl.loop(0, TAPS)
+    def _(t):
+        for a in range(3):
+            turned = w_ref[9 * a + t].astype(F32).T.astype(BF16)
+            at = pl.ds(pl.multiple_of(t * ci, ci), ci)
+            wf[0, at, a * ci : (a + 1) * ci] = turned[:ci]
+            wf[1, at, a * ci : (a + 1) * ci] = turned[ci:]
+
+    cot_x.wait_recv()
+
+    @pl.when(has_next)
+    def _():
+        f_next.start()
+
+    @pl.when(has_prev)
+    def _():
+        f_prev.start()
+
+    @pl.when(has_prev)
+    def _():
+        x_next.wait_recv()
+
+    @pl.when(has_next)
+    def _():
+        x_prev.wait_recv()
+
+    keep, begin = [], 0
+    for b in range(levels):
+        size = rows3 >> (b + 1)
+        keep.append((begin + bits[b] * size, begin + (1 - bits[b]) * size, size))
+        begin = begin + bits[b] * size
+
+    def span(at, size):
+        return pl.ds(pl.multiple_of(at, 8), size)
+
+    def step_copy(j, stage):
+        if stage < levels:
+            b = stage
+            _, away, size = keep[b]
+            src, dst = part.at[j, span(away, size)], bufs[b].at[j]
+        else:
+            b = 2 * levels - 1 - stage
+            own, _, size = keep[b]
+            src = dst = wg_ref.at[j, span(own, size)]
+        return pltpu.make_async_remote_copy(
+            src_ref=src, dst_ref=dst, send_sem=gs.at[stage, j], recv_sem=gr.at[stage, j],
+            device_id=(mates[b], h), device_id_type=MESH,
+        )
+
+    def advance(j, stage):
+        step_copy(j, stage).wait_recv()
+        if stage < levels:
+            own, _, size = keep[stage]
+            at = span(own, size)
+            into = part if stage < levels - 1 else wg_ref
+            into[j, at, :] = part[j, at, :] + bufs[stage][j]
+        if stage + 1 < 2 * levels:
+            step_copy(j, stage + 1).start()
+
+    stage_of = {}
+
+    def pump():
+        for j in sorted(stage_of):
+            if stage_of[j] < 2 * levels:
+                advance(j, stage_of[j])
+                stage_of[j] += 1
+
+    for t in range(TAPS):
+        b, c = t // 3, t % 3
+
+        @pl.loop(0, co // 32)
+        def _(i, t=t, b=b, c=c):
+            at = pl.multiple_of(i * 32, 32)
+            value = c3[pl.ds(co + at, 32), :].astype(F32)
+            cs[t % 2, pl.ds(at, 32), :] = moved(value, b - 1, c - 1).astype(BF16)
+
+        part[t] = lax.dot_general(
+            x3[...], cs[t % 2], (((1,), (1,)), ((), ())), preferred_element_type=F32
+        )
+        if t >= 1:
+            pump()
+        step_copy(t, 0).start()
+        stage_of[t] = 0
+
+    def products(pairs):
+        @pl.loop(0, cells // 256)
+        def _(i):
+            at = pl.ds(pl.multiple_of(i * 256, 256), 256)
+            total = None
+            for left, right in pairs:
+                term = jnp.dot(left(), right(at), preferred_element_type=F32)
+                total = term if total is None else total + term
+            z[:, at] = total
+
+    def collect(store, sign):
+        @pl.loop(0, ci // 8)
+        def _(i):
+            total = None
+            for c in range(3):
+                line = None
+                for b in range(3):
+                    at = pl.ds(pl.multiple_of((b * 3 + c) * ci + i * 8, 8), 8)
+                    piece = moved(z[at, :], sign * (b - 1), 0)
+                    line = piece if line is None else line + piece
+                line = moved(line, 0, sign * (c - 1))
+                total = line if total is None else total + line
+            store(pl.ds(pl.multiple_of(i * 8, 8), 8), total)
+
+    def put(ref):
+        def store(at, value):
+            ref[at, :] = value
+
+        return store
+
+    products([(lambda: wf[other], lambda at: x3[:, at])])
+    pump()
+    collect(put(theirs), -1)
+    share.start()
+    pump()
+    products([(lambda: wf[h], lambda at: x3[:, at])])
+    pump()
+    collect(put(mine), -1)
+    pump()
+
+    @pl.when(has_prev)
+    def _():
+        c_next.wait_recv()
+        f_next.wait_recv()
+
+    @pl.when(has_next)
+    def _():
+        c_prev.wait_recv()
+        f_prev.wait_recv()
+
+    products([
+        (
+            lambda a=a: w_ref[9 * a : 9 * a + 9].reshape(TAPS * ci, co),
+            lambda at, a=a: c3[pl.ds(a * co, co), at],
+        )
+        for a in range(3)
+    ])
+    pump()
+
+    share.wait_recv()
+    total_out = mine[...] + rx[...]
+    out_ref[...] = total_out.astype(BF16)
+    collect(put(mine), 1)
+    grad_ref[...] = mine[...].astype(BF16)
+    pump()
+    while any(stage_of[j] < 2 * levels for j in stage_of):
+        pump()
+
+    cot_x.wait_send()
+    share.wait_send()
+
+    @pl.when(has_next)
+    def _():
+        x_next.wait_send()
+        c_next.wait_send()
+        f_next.wait_send()
+
+    @pl.when(has_prev)
+    def _():
+        x_prev.wait_send()
+        c_prev.wait_send()
+        f_prev.wait_send()
+
+    for t in range(TAPS):
+        for stage in range(2 * levels):
+            step_copy(t, stage).wait_send()
+
+
+def fused(count, levels, inputs, weights, cotangent):
+    ci, cells = inputs.shape[1:]
+    co = weights.shape[2]
+    rows3 = 3 * ci
+    vmem = pl.BlockSpec(memory_space=pltpu.VMEM)
+    out, grad, wg = pl.pallas_call(
+        functools.partial(kernel, count, levels),
+        out_shape=(
+            jax.ShapeDtypeStruct((ci, cells), BF16),
+            jax.ShapeDtypeStruct((ci, cells), BF16),
+            jax.ShapeDtypeStruct((TAPS, rows3, co), F32),
+        ),
+        in_specs=[vmem] * 3,
+        out_specs=(vmem,) * 3,
+        scratch_shapes=[
+            pltpu.VMEM((rows3, cells), BF16),
+            pltpu.VMEM((3 * co, cells), BF16),
+            pltpu.VMEM((2, TAPS * ci, rows3), BF16),
+            pltpu.VMEM((2, co, cells), BF16),
+            pltpu.VMEM((TAPS * ci, cells), F32),
+            pltpu.VMEM((ci, cells), F32),
+            pltpu.VMEM((ci, cells), F32),
+            pltpu.VMEM((ci, cells), F32),
+            pltpu.VMEM((TAPS, rows3, co), F32),
+        ]
+        + [pltpu.VMEM((TAPS, rows3 >> (b + 1), co), F32) for b in range(levels)]
+        + [
+            pltpu.SemaphoreType.DMA((8,)),
+            pltpu.SemaphoreType.DMA((8,)),
+            pltpu.SemaphoreType.DMA((2 * levels, TAPS)),
+            pltpu.SemaphoreType.DMA((2 * levels, TAPS)),
+        ],
+        compiler_params=pltpu.CompilerParams(
+            collective_id=0, has_side_effects=True, vmem_limit_bytes=58 * 2**20
+        ),
+        cost_estimate=pl.CostEstimate(
+            flops=6 * 27 * ci * co * cells, bytes_accessed=8 * 2**20, transcendentals=0
+        ),
+    )(inputs[0], weights, cotangent[0])
+    wg = wg.reshape(TAPS, 3, ci, co).transpose(1, 0, 2, 3).reshape(27, ci, co)
+    return out[None], grad[None], wg
+
+
+def local_any(count, groups, inputs, weights, cotangent):
+    levels = count.bit_length() - 1
+    planes, ci, _ = inputs.shape
+    fits = planes == 1 and groups == 2 and 2 * ci == weights.shape[2] and ci % 128 == 0
+    if fits and count == 1 << levels and (3 * ci) % (8 * count) == 0:
+        return fused(count, levels, inputs, weights, cotangent)
+    return local(inputs, weights, cotangent)
+
+
 def solution(mesh):
     placed = (P("space", "chan", None), P(None, "chan", None), P("space", "chan", None))
     return jax.shard_map(
-        local,
+        functools.partial(local_any, mesh.shape["space"], mesh.shape["chan"]),
         mesh=mesh,
         in_specs=placed,
         out_specs=(P("space", "chan", None), P("space", "chan", None), P(None, "chan", None)),

time: 202 us -> 120 us (0.59)
  Pallas kernels: 0 us -> 113 us
  waiting for transfers between devices: 78.3 us -> 0 us
  local copies, waits for them, and re-layouts: 51.3 us -> 5.85 us
  matrix products: 40.9 us -> 0 us
  between operations: 14.8 us -> 0.66 us
  starting transfers between devices: 11.1 us -> 0 us
  other arithmetic: 4.45 us -> 0 us
    pallas_call x0 -> x1, Pallas kernels: none -> 113 us  [fused(): pl.pallas_call(functools.partial(kernel, count, levels), out_shape=(jax.S...]
    psum x1 -> x0, waiting for transfers between devices: 72.2 us -> none  [local(): weight_grad = lax.psum(local_terms, 'space')]
    dot_general x27 -> x0, matrix products: 40.9 us -> none  [the longest x18 23 us: convolve(): jnp.einsum('dcp,co->dop', stack_at(padded, tap_row, tap_col), tap_weights...]
    unnamed x179 -> x6, local copies, waits for them, and re-layouts: 29.5 us -> 1.59 us
    slice x4 -> x0, local copies, waits for them, and re-layouts: 18.1 us -> none  [stack_at(): moved[tap_depth:tap_depth + planes]]
    ppermute x4 -> x0, starting transfers between devices: 10.8 us -> none  [the longest x2 8.24 us: extended(): lax.ppermute(lax.slice_in_dim(block, block.shape[dim] - width, None, axis...]
    all_gather x1 -> x0, waiting for transfers between devices: 6.04 us -> none  [local(): gathered = lax.all_gather(cotangent, 'chan', axis=1, tiled=True)]
    transpose x1, local copies, waits for them, and re-layouts: 0.12 us -> 4.26 us  [fused(): wg = wg.reshape(TAPS, 3, ci, co).transpose(1, 0, 2, 3).reshape(27, ci, co)]
  transfers between devices with their start and end apart: 7 -> 0, of which waited for: 2 -> 0; matrix products, arithmetic and copies ran while one was open for 43% -> 0% of each run, Pallas kernels for 0% -> 0%
where the time goes in v1:
time: 120 us; the launch traced here: 119 us
  Pallas kernels  113 us (94%)
  local copies, waits for them, and re-layouts  5.85 us (5%)
    pallas_call x1, Pallas kernels, fused(): pl.pallas_call(functools.partial(kernel, count, levels), out_shape=(jax.S...  113 us
    transpose x1, local copies, waits for them, and re-layouts, fused(): wg = wg.reshape(TAPS, 3, ci, co).transpose(1, 0, 2, 3).reshape(27, ci, co)  4.26 us

profile of v1, /device:TPU:0, one launch (start us, length us, event | category | flops | bytes accessed | tf_op | source)
XLA Modules:
  0.0 119.4 jit_solution(5243412380606591092)
XLA Ops:
  0.6 112.9 %shard_map.58 = (bf16[128,2048]{1,0:T(8,128)(2,1)}, bf16[128,2048]{1,0:T(8,128)(2,1)}, f32[9,384,256]{2,1,0:T(8,128)}) custom-call(bf16[128,2048]{1,0:T(8,128)(2,1)} %bitcast.12, bf16[27,128,256]{2,1,0:T(8,128)(2,1)} %w_ref.1, bf16[128,2048]{1,0:T(8,128)(2,1)} %bitcast.13), custom_call_target="tpu_custom_call" | custom-call | flops 10871635968 | bytes 8388608 | tf_op jit(solution)/shard_map/pallas_call | solution.py:374
  113.5 0.0 copy-start.1
  113.5 0.0 copy-start
  113.6 4.3 %copy.6 = f32[3,9,128,256]{3,2,1,0:T(8,128)} copy(f32[3,9,128,256]{3,2,0,1:T(8,128)} %bitcast.9) | data formatting | bytes 7077888 | tf_op jit(solution)/shard_map/transpose | solution.py:408
  117.8 0.0 copy-done.1
  117.8 0.8 copy.9
  118.6 0.0 copy-done
  118.6 0.8 copy.10
Async XLA Ops:
  113.5 4.3 %copy-start.1 = (bf16[128,2048]{1,0:T(8,128)(2,1)S(1)}, bf16[128,2048]{1,0:T(8,128)(2,1)}, u32[]{:S(2)}) copy-start(bf16[128,2048]{1,0:T(8,128)(2,1)} %get-tuple-element.6) | copy-start | bytes 1572868
  113.5 5.1 %copy-start = (bf16[128,2048]{1,0:T(8,128)(2,1)S(1)}, bf16[128,2048]{1,0:T(8,128)(2,1)}, u32[]{:S(2)}) copy-start(bf16[128,2048]{1,0:T(8,128)(2,1)} %get-tuple-element.7) | copy-start | bytes 1572868

commit v2 on v1

--- a/solution.py
+++ b/solution.py
@@ -96,6 +96,7 @@
     return (output, input_grad, weight_grad)
 
 
+GROUPS = 2
 TAPS = 9
 
 
@@ -253,33 +254,51 @@
         if stage + 1 < 2 * levels:
             step_copy(j, stage + 1).start()
 
-    stage_of = {}
+    stage_of, order = {}, []
 
     def pump():
-        for j in sorted(stage_of):
-            if stage_of[j] < 2 * levels:
+        turn = len(order)
+        order.append(turn)
+        for place, j in enumerate(stage_of):
+            if place % GROUPS == turn % GROUPS and stage_of[j] < 2 * levels:
                 advance(j, stage_of[j])
                 stage_of[j] += 1
 
-    for t in range(TAPS):
-        b, c = t // 3, t % 3
+    pad = jnp.zeros((ROW_CELLS, co), BF16)
+    for c in range(3):
+        cs[c, pl.ds(0, ROW_CELLS), :] = pad
+        cs[c, pl.ds(ROW_CELLS + cells, ROW_CELLS), :] = pad
 
         @pl.loop(0, co // 32)
-        def _(i, t=t, b=b, c=c):
+        def _(i, c=c):
             at = pl.multiple_of(i * 32, 32)
             value = c3[pl.ds(co + at, 32), :].astype(F32)
-            cs[t % 2, pl.ds(at, 32), :] = moved(value, b - 1, c - 1).astype(BF16)
-
-        part[t] = lax.dot_general(
-            x3[...], cs[t % 2], (((1,), (1,)), ((), ())), preferred_element_type=F32
-        )
-        if t >= 1:
+            z[pl.ds(at, 32), :] = moved(value, 0, c - 1)
+
+        @pl.loop(0, cells // 256)
+        def _(i, c=c):
+            at = pl.multiple_of(i * 256, 256)
+            turned = z[pl.ds(0, co), pl.ds(at, 256)].T.astype(BF16)
+            cs[c, pl.ds(pl.multiple_of(at + ROW_CELLS, 64), 256), :] = turned
+
+        for b in range(3):
+            t = 3 * b + c
+            part[t] = jnp.dot(
+                x3[...], cs[c, pl.ds((2 - b) * ROW_CELLS, cells), :], preferred_element_type=F32
+            )
             pump()
-        step_copy(t, 0).start()
-        stage_of[t] = 0
+            step_copy(t, 0).start()
+            stage_of[t] = 0
 
     def products(pairs):
-        @pl.loop(0, cells // 256)
+        tiles = cells // 256
+        for first in range(0, tiles, 2):
+            products_of(pairs, first, first + 2)
+            if first + 2 < tiles:
+                pump()
+
+    def products_of(pairs, first, last):
+        @pl.loop(first, last)
         def _(i):
             at = pl.ds(pl.multiple_of(i * 256, 256), 256)
             total = None
@@ -289,7 +308,13 @@
             z[:, at] = total
 
     def collect(store, sign):
-        @pl.loop(0, ci // 8)
+        strips = ci // 8
+        collect_of(store, sign, 0, strips // 2)
+        pump()
+        collect_of(store, sign, strips // 2, strips)
+
+    def collect_of(store, sign, first, last):
+        @pl.loop(first, last)
         def _(i):
             total = None
             for c in range(3):
@@ -384,7 +409,7 @@
             pltpu.VMEM((rows3, cells), BF16),
             pltpu.VMEM((3 * co, cells), BF16),
             pltpu.VMEM((2, TAPS * ci, rows3), BF16),
-            pltpu.VMEM((2, co, cells), BF16),
+            pltpu.VMEM((3, cells + 2 * ROW_CELLS, co), BF16),
             pltpu.VMEM((TAPS * ci, cells), F32),
             pltpu.VMEM((ci, cells), F32),
             pltpu.VMEM((ci, cells), F32),

time: 120 us -> 106 us (0.88)
  Pallas kernels: 113 us -> 99.1 us
    pallas_call x1, Pallas kernels: 113 us -> 99.1 us  [fused(): pl.pallas_call(functools.partial(kernel, count, levels), out_shape=(jax.S...]
where the time goes in v2:
time: 106 us
  Pallas kernels  99.1 us (93%)
  local copies, waits for them, and re-layouts  5.85 us (6%)
    pallas_call x1, Pallas kernels, fused(): pl.pallas_call(functools.partial(kernel, count, levels), out_shape=(jax.S...  99.1 us
    transpose x1, local copies, waits for them, and re-layouts, fused(): wg = wg.reshape(TAPS, 3, ci, co).transpose(1, 0, 2, 3).reshape(27, ci, co)  4.26 us

profile of v2, /device:TPU:0, one launch (start us, length us, event | category | flops | bytes accessed | tf_op | source)
XLA Modules:
  0.0 105.6 jit_solution(2831983140334239213)
XLA Ops:
  0.6 99.1 %shard_map.58 = (bf16[128,2048]{1,0:T(8,128)(2,1)}, bf16[128,2048]{1,0:T(8,128)(2,1)}, f32[9,384,256]{2,1,0:T(8,128)}) custom-call(bf16[128,2048]{1,0:T(8,128)(2,1)} %bitcast.12, bf16[27,128,256]{2,1,0:T(8,128)(2,1)} %w_ref.1, bf16[128,2048]{1,0:T(8,128)(2,1)} %bitcast.13), custom_call_target="tpu_custom_call" | custom-call | flops 10871635968 | bytes 8388608 | tf_op jit(solution)/shard_map/pallas_call | solution.py:399
  99.7 0.0 copy-start.1
  99.8 0.0 copy-start
  99.8 4.3 %copy.6 = f32[3,9,128,256]{3,2,1,0:T(8,128)} copy(f32[3,9,128,256]{3,2,0,1:T(8,128)} %bitcast.9) | data formatting | bytes 7077888 | tf_op jit(solution)/shard_map/transpose | solution.py:433
  104.0 0.0 copy-done.1
  104.0 0.8 copy.9
  104.8 0.0 copy-done
  104.8 0.8 copy.10
Async XLA Ops:
  99.7 4.3 %copy-start.1 = (bf16[128,2048]{1,0:T(8,128)(2,1)S(1)}, bf16[128,2048]{1,0:T(8,128)(2,1)}, u32[]{:S(2)}) copy-start(bf16[128,2048]{1,0:T(8,128)(2,1)} %get-tuple-element.6) | copy-start | bytes 1572868
  99.8 5.1 %copy-start = (bf16[128,2048]{1,0:T(8,128)(2,1)S(1)}, bf16[128,2048]{1,0:T(8,128)(2,1)}, u32[]{:S(2)}) copy-start(bf16[128,2048]{1,0:T(8,128)(2,1)} %get-tuple-element.7) | copy-start | bytes 1572868
